TPU v7x, 32 devices: a whole 2x2x4 slice. The times are simulated.
32 devices in a mesh: fsdp: 2 (over y), replica: 16 (over z, x, core).
Axes of the slice: x: 2, y: 2, z: 4, core: 2. Of those that a mesh axis runs over, the one named last changes fastest.
Arguments:
- inputs: bfloat16 [16, 1024, 960], P('replica', 'fsdp'), may hold values from -6 to 6
- segment_ids: int32 [16, 1024], P('replica'), may hold values from 0 to 1, as said below
- positions: int32 [16, 1024], P('replica', 'fsdp'), may hold values from 0 to 1023, as said below
- attn_gain: bfloat16 [960], P('fsdp'), may hold values from 0.099609375 to 1.8984375
- q_weight: bfloat16 [960, 960], P('fsdp'), may hold values from -0.25 to 0.25
- key_matrix: bfloat16 [320, 960], P('fsdp'), may hold values from -0.25 to 0.25
- value_matrix: bfloat16 [320, 960], P('fsdp'), may hold values from -0.1875 to 0.1875
- o_weight: bfloat16 [960, 960], P('fsdp'), may hold values from -1.5 to 1.5
- ffn_gain: bfloat16 [960], P('fsdp'), may hold values from 0.099609375 to 1.8984375
- gate_weight: bfloat16 [2560, 960], P('fsdp'), may hold values from -0.1875 to 0.1875
- up_weight: bfloat16 [2560, 960], P('fsdp'), may hold values from -0.1875 to 0.1875
- down_weight: bfloat16 [2560, 960], P('fsdp'), may hold values from -0.125 to 0.125
- cotangent: bfloat16 [16, 1024, 960], P('replica', 'fsdp'), may hold values from -6 to 6
Outputs:
- outputs: bfloat16 [16, 1024, 960], P('replica', 'fsdp')
- input_grad: float32 [16, 1024, 960], P('replica', 'fsdp')
- attn_gain_grad: float32 [960], P('fsdp')
- q_weight_grad: float32 [960, 960], P('fsdp')
- k_weight_grad: float32 [320, 960], P('fsdp')
- v_weight_grad: float32 [320, 960], P('fsdp')
- o_weight_grad: float32 [960, 960], P('fsdp')
- ffn_gain_grad: float32 [960], P('fsdp')
- gate_weight_grad: float32 [2560, 960], P('fsdp')
- up_weight_grad: float32 [2560, 960], P('fsdp')
- down_weight_grad: float32 [2560, 960], P('fsdp')
Inputs may be any that keep to these rules, and one draw needn't show every extreme that they name: `segment_ids`: in each sequence the first h tokens have number 0 and the rest number 1, with h from 128 to 384. Within a document positions rise by one from token to token; the document numbered 1 starts at position 0.
All inputs are finite; a program needn't handle non-finite values.
Results may differ from a plain program's by a relative error of at most 0.023.
Values may be sent and summed in bfloat16 or wider, within the bound.
A program may use at most 256 MiB of HBM per device.

v0:
```python
import jax
import jax.numpy as jnp
from jax import lax
from jax.sharding import PartitionSpec as P

QUERY_HEADS = 15
KEY_VALUE_HEADS = 5
HEAD_SIZE = 64


norm_eps = 1e-05
rotary_base = 100000.0


def normalize_parts(value_rows):
    factor = lax.rsqrt(jnp.mean(value_rows * value_rows, axis=-1, keepdims=True) + norm_eps)
    return (value_rows * factor, factor)


def norm_back(upstream, normed, factor):
    return factor * (upstream - normed * jnp.mean(upstream * normed, axis=-1, keepdims=True))


def project_rows(left, weight):
    return lax.dot_general(
        left, weight, (((1,), (1,)), ((), ())), preferred_element_type=jnp.float32
    )


def contract_rows(left, right):
    return lax.dot_general(
        left, right, (((0,), (0,)), ((), ())), preferred_element_type=jnp.float32
    )


def rotary_tables(positions):
    half = HEAD_SIZE // 2
    frequency = rotary_base ** (-(jnp.arange(half, dtype=jnp.float32) * 2.0 / HEAD_SIZE))
    angles = positions.astype(jnp.float32)[:, None] * frequency[None, :]
    cosine_table = jnp.concatenate([jnp.cos(angles), jnp.cos(angles)], axis=-1)[:, None, :]
    sine_table = jnp.concatenate([jnp.sin(angles), jnp.sin(angles)], axis=-1)[:, None, :]
    return (cosine_table, sine_table)


def apply_rotary(field, cosine_table, sine_table):
    half = HEAD_SIZE // 2
    turned = jnp.concatenate([-field[..., half:], field[..., :half]], axis=-1)
    return field * cosine_table + turned * sine_table


def apply_rotary_back(field, cosine_table, sine_table):
    half = HEAD_SIZE // 2
    scaled = field * sine_table
    turned = jnp.concatenate([scaled[..., half:], -scaled[..., :half]], axis=-1)
    return field * cosine_table + turned


def swiglu_back(active_back, gate, up):
    sigma = jax.nn.sigmoid(gate)
    gate_back = (active_back * up * sigma * (1.0 + gate * (1.0 - sigma))).astype(jnp.bfloat16)
    up_back = (active_back * gate * sigma).astype(jnp.bfloat16)
    return (gate_back, up_back)


def masked_scores(query_rotated, gathered_keys, allowed):
    token_rows = query_rotated.shape[0]
    grouped_heads = query_rotated.reshape(
        token_rows, KEY_VALUE_HEADS, QUERY_HEADS // KEY_VALUE_HEADS, HEAD_SIZE
    )
    keyed_rows = gathered_keys.reshape(gathered_keys.shape[0], KEY_VALUE_HEADS, HEAD_SIZE)
    scores = jnp.einsum(
        "qkrd,skd->krqs", grouped_heads, keyed_rows, preferred_element_type=jnp.float32
    ) * HEAD_SIZE ** (-0.5)
    return jnp.where(allowed[None, None], scores, -1e30)


def on_device(
    inputs,
    segment_ids,
    positions,
    attn_gain,
    q_weight,
    key_matrix,
    value_matrix,
    o_weight,
    ffn_gain,
    gate_weight,
    up_weight,
    down_weight,
    cotangent,
):
    token_rows = inputs.shape[1]
    scale = HEAD_SIZE ** (-0.5)
    first = lax.axis_index("fsdp") * token_rows
    data = inputs[0].astype(jnp.float32)
    segments = segment_ids[0]
    sequence_length = segments.shape[0]
    cosine_table, sine_table = rotary_tables(positions[0])
    query_full, key_complete, value_full, out_full, gain_first, gain_second = (
        lax.all_gather(q_weight, "fsdp", axis=0, tiled=True),
        lax.all_gather(key_matrix, "fsdp", axis=0, tiled=True),
        lax.all_gather(value_matrix, "fsdp", axis=0, tiled=True),
        lax.all_gather(o_weight, "fsdp", axis=0, tiled=True),
        lax.all_gather(attn_gain, "fsdp", axis=0, tiled=True),
        lax.all_gather(ffn_gain, "fsdp", axis=0, tiled=True),
    )
    gain_first = gain_first.astype(jnp.float32)
    gain_second = gain_second.astype(jnp.float32)
    normed, factor_one = normalize_parts(data)
    hidden_state = (normed * gain_first).astype(jnp.bfloat16)
    query_rotated = apply_rotary(
        project_rows(hidden_state, query_full).reshape(token_rows, QUERY_HEADS, HEAD_SIZE),
        cosine_table,
        sine_table,
    ).astype(jnp.bfloat16)
    key_rotated = apply_rotary(
        project_rows(hidden_state, key_complete).reshape(token_rows, KEY_VALUE_HEADS, HEAD_SIZE),
        cosine_table,
        sine_table,
    ).astype(jnp.bfloat16)
    value_low = project_rows(hidden_state, value_full).astype(jnp.bfloat16)
    gathered_keys, gathered_values = (
        lax.all_gather(
            key_rotated.reshape(token_rows, KEY_VALUE_HEADS * HEAD_SIZE), "fsdp", axis=0, tiled=True
        ),
        lax.all_gather(value_low, "fsdp", axis=0, tiled=True),
    )
    query_index = first + jnp.arange(token_rows)
    own_segments = lax.dynamic_slice_in_dim(segments, first, token_rows)
    allowed = (own_segments[:, None] == segments[None, :]) & (
        query_index[:, None] >= jnp.arange(sequence_length)[None, :]
    )
    scores = masked_scores(query_rotated, gathered_keys, allowed)
    top = jnp.max(scores, axis=-1, keepdims=True)
    raised = jnp.exp(scores - top)
    total = jnp.sum(raised, axis=-1, keepdims=True)
    attention_step = (raised / total).astype(jnp.bfloat16)
    log_total = top + jnp.log(total)
    value_rows_gathered = gathered_values.reshape(sequence_length, KEY_VALUE_HEADS, HEAD_SIZE)
    mixed_output = jnp.einsum(
        "nluh,hng->unlg", attention_step, value_rows_gathered, preferred_element_type=jnp.float32
    )
    mixed_low = mixed_output.reshape(token_rows, QUERY_HEADS * HEAD_SIZE).astype(jnp.bfloat16)
    middle = data + project_rows(mixed_low, out_full)
    normed_two, factor_two = normalize_parts(middle)
    hidden_two = (normed_two * gain_second).astype(jnp.bfloat16)
    back_out = cotangent[0].astype(jnp.float32)
    down_back = back_out.astype(jnp.bfloat16)
    every_hidden = lax.all_gather(hidden_two, "fsdp", axis=0, tiled=True)
    gate = project_rows(every_hidden, gate_weight)
    up = project_rows(every_hidden, up_weight)
    active = (gate * jax.nn.sigmoid(gate) * up).astype(jnp.bfloat16)
    down = lax.psum_scatter(
        jnp.dot(active, down_weight, preferred_element_type=jnp.float32).astype(jnp.bfloat16),
        "fsdp",
        scatter_dimension=0,
        tiled=True,
    ).astype(jnp.float32)
    result = middle + down
    every_back = lax.all_gather(down_back, "fsdp", axis=0, tiled=True)
    gate_back, up_back = swiglu_back(project_rows(every_back, down_weight), gate, up)
    partial_back = jnp.dot(gate_back, gate_weight, preferred_element_type=jnp.float32) + jnp.dot(
        up_back, up_weight, preferred_element_type=jnp.float32
    )
    hidden_two_back = lax.psum_scatter(
        partial_back.astype(jnp.bfloat16), "fsdp", scatter_dimension=0, tiled=True
    ).astype(jnp.float32)
    gate_sum = contract_rows(gate_back, every_hidden)
    up_sum = contract_rows(up_back, every_hidden)
    down_sum = contract_rows(active, every_back)
    outputs = result.astype(jnp.bfloat16)[None]
    gate_sum, up_sum, down_sum = (
        lax.psum(gate_sum.astype(jnp.bfloat16), "replica").astype(jnp.float32),
        lax.psum(up_sum.astype(jnp.bfloat16), "replica").astype(jnp.float32),
        lax.psum(down_sum.astype(jnp.bfloat16), "replica").astype(jnp.float32),
    )
    gain_second_term = jnp.sum(hidden_two_back * normed_two, axis=0)
    middle_back = back_out + norm_back(hidden_two_back * gain_second, normed_two, factor_two)
    attn_back = middle_back.astype(jnp.bfloat16)
    mixed_output_back = jnp.dot(attn_back, out_full, preferred_element_type=jnp.float32).astype(
        jnp.bfloat16
    )
    out_term = contract_rows(attn_back, mixed_low)
    scores = masked_scores(query_rotated, gathered_keys, allowed)
    attend_full = jnp.exp(scores - log_total)
    attention_step = attend_full.astype(jnp.bfloat16)
    grouped_heads_back = mixed_output_back.reshape(
        token_rows, KEY_VALUE_HEADS, QUERY_HEADS // KEY_VALUE_HEADS, HEAD_SIZE
    )
    attend_back = jnp.einsum(
        "qkrd,skd->krqs",
        grouped_heads_back,
        value_rows_gathered,
        preferred_element_type=jnp.float32,
    )
    value_term = jnp.einsum(
        "krqs,qkrd->skd", attention_step, grouped_heads_back, preferred_element_type=jnp.float32
    ).reshape(sequence_length, KEY_VALUE_HEADS * HEAD_SIZE)
    score_back = (
        attend_full * (attend_back - jnp.sum(attend_full * attend_back, axis=-1, keepdims=True))
    ).astype(jnp.bfloat16)
    key_rows_gathered = gathered_keys.reshape(sequence_length, KEY_VALUE_HEADS, HEAD_SIZE)
    query_by_group = query_rotated.reshape(
        token_rows, KEY_VALUE_HEADS, QUERY_HEADS // KEY_VALUE_HEADS, HEAD_SIZE
    )
    query_rot_back = (
        jnp.einsum(
            "nluh,hng->unlg", score_back, key_rows_gathered, preferred_element_type=jnp.float32
        ).reshape(token_rows, QUERY_HEADS, HEAD_SIZE)
        * scale
    )
    key_term = (
        jnp.einsum(
            "krqs,qkrd->skd", score_back, query_by_group, preferred_element_type=jnp.float32
        ).reshape(sequence_length, KEY_VALUE_HEADS * HEAD_SIZE)
        * scale
    )
    key_local, value_owned = (
        lax.psum_scatter(
            key_term.astype(jnp.bfloat16), "fsdp", scatter_dimension=0, tiled=True
        ).astype(jnp.float32),
        lax.psum_scatter(
            value_term.astype(jnp.bfloat16), "fsdp", scatter_dimension=0, tiled=True
        ).astype(jnp.float32),
    )
    query_back = (
        apply_rotary_back(query_rot_back, cosine_table, sine_table)
        .reshape(token_rows, QUERY_HEADS * HEAD_SIZE)
        .astype(jnp.bfloat16)
    )
    key_back = (
        apply_rotary_back(
            key_local.reshape(token_rows, KEY_VALUE_HEADS, HEAD_SIZE), cosine_table, sine_table
        )
        .reshape(token_rows, KEY_VALUE_HEADS * HEAD_SIZE)
        .astype(jnp.bfloat16)
    )
    value_back = value_owned.astype(jnp.bfloat16)
    hidden_back = (
        jnp.dot(query_back, query_full, preferred_element_type=jnp.float32)
        + jnp.dot(key_back, key_complete, preferred_element_type=jnp.float32)
        + jnp.dot(value_back, value_full, preferred_element_type=jnp.float32)
    )
    gain_first_term = jnp.sum(hidden_back * normed, axis=0)
    input_back = middle_back + norm_back(hidden_back * gain_first, normed, factor_one)
    query_sum, key_sum, value_sum, out_sum, gain_first_sum, gain_second_sum = (
        lax.psum_scatter(
            contract_rows(query_back, hidden_state).astype(jnp.bfloat16),
            "fsdp",
            scatter_dimension=0,
            tiled=True,
        ).astype(jnp.float32),
        lax.psum_scatter(
            contract_rows(key_back, hidden_state).astype(jnp.bfloat16),
            "fsdp",
            scatter_dimension=0,
            tiled=True,
        ).astype(jnp.float32),
        lax.psum_scatter(
            contract_rows(value_back, hidden_state).astype(jnp.bfloat16),
            "fsdp",
            scatter_dimension=0,
            tiled=True,
        ).astype(jnp.float32),
        lax.psum_scatter(
            out_term.astype(jnp.bfloat16), "fsdp", scatter_dimension=0, tiled=True
        ).astype(jnp.float32),
        lax.psum_scatter(
            gain_first_term.astype(jnp.bfloat16), "fsdp", scatter_dimension=0, tiled=True
        ).astype(jnp.float32),
        lax.psum_scatter(
            gain_second_term.astype(jnp.bfloat16), "fsdp", scatter_dimension=0, tiled=True
        ).astype(jnp.float32),
    )
    query_sum, key_sum, value_sum, out_sum, gain_first_sum, gain_second_sum = (
        lax.psum(query_sum.astype(jnp.bfloat16), "replica").astype(jnp.float32),
        lax.psum(key_sum.astype(jnp.bfloat16), "replica").astype(jnp.float32),
        lax.psum(value_sum.astype(jnp.bfloat16), "replica").astype(jnp.float32),
        lax.psum(out_sum.astype(jnp.bfloat16), "replica").astype(jnp.float32),
        lax.psum(gain_first_sum.astype(jnp.bfloat16), "replica").astype(jnp.float32),
        lax.psum(gain_second_sum.astype(jnp.bfloat16), "replica").astype(jnp.float32),
    )
    return (
        outputs,
        input_back[None],
        gain_first_sum,
        query_sum,
        key_sum,
        value_sum,
        out_sum,
        gain_second_sum,
        gate_sum,
        up_sum,
        down_sum,
    )


def solution(mesh):
    in_specs = (
        P("replica", "fsdp", None),
        P("replica", None),
        P("replica", "fsdp"),
        P("fsdp"),
        P("fsdp", None),
        P("fsdp", None),
        P("fsdp", None),
        P("fsdp", None),
        P("fsdp"),
        P("fsdp", None),
        P("fsdp", None),
        P("fsdp", None),
        P("replica", "fsdp", None),
    )
    out_specs = (
        P("replica", "fsdp", None),
        P("replica", "fsdp", None),
        P("fsdp"),
        P("fsdp", None),
        P("fsdp", None),
        P("fsdp", None),
        P("fsdp", None),
        P("fsdp"),
        P("fsdp", None),
        P("fsdp", None),
        P("fsdp", None),
    )
    return jax.shard_map(
        on_device, mesh=mesh, in_specs=in_specs, out_specs=out_specs, check_vma=False
    )
```

profile of v0, /device:TPU:0, one launch (start us, length us, event | category | flops | bytes accessed | tf_op | source)
XLA Modules:
  0.0 697.8 jit_solution(109520022649959368)
XLA Ops:
  10.9 5.8 all-reduce.7
  16.8 16.8 %all_gather.33 = bf16[320,960]{1,0:T(8,128)(2,1)S(1)} all-gather(bf16[160,960]{1,0:T(8,128)(2,1)} %param.18), channel_id=1, replica_groups=mesh['fsdp'=2,'replica'=16] {'fsdp'}, dimensions={0}, use_global_device_ids=true | all-gather | bytes 921600 | tf_op jit(solution)/shard_map/all_gather | solution.py:101
  33.5 17.0 %all_gather.31 = bf16[320,960]{1,0:T(8,128)(2,1)S(1)} all-gather(bf16[160,960]{1,0:T(8,128)(2,1)} %param.19), channel_id=1, replica_groups=mesh['fsdp'=2,'replica'=16] {'fsdp'}, dimensions={0}, use_global_device_ids=true | all-gather | bytes 921600 | tf_op jit(solution)/shard_map/all_gather | solution.py:102
  52.0 9.5 %all_gather.32 = bf16[1024,320]{0,1:T(8,128)(2,1)} all-gather(bf16[512,320]{0,1:T(8,128)(2,1)S(1)} %convolution_convert_fusion.9), channel_id=1, replica_groups=mesh['fsdp'=2,'replica'=16] {'fsdp'}, dimensions={0}, use_global_device_ids=true | all-gather | bytes 983040 | tf_op jit(solution)/shard_map/all_gather | solution.py:126
  63.3 11.6 %all_gather.34 = bf16[1024,320]{0,1:T(8,128)(2,1)} all-gather(bf16[512,320]{0,1:T(8,128)(2,1)S(1)} %bitcast.194), channel_id=1, replica_groups=mesh['fsdp'=2,'replica'=16] {'fsdp'}, dimensions={0}, use_global_device_ids=true | all-gather | bytes 983040 | tf_op jit(solution)/shard_map/all_gather | solution.py:123
  81.3 12.6 %fusion.71 = (f32[5,3,512]{2,1,0:T(4,128)S(1)}, f32[5,3,512,1024]{2,3,1,0:T(8,128)}) fusion(bf16[1024,5,64,1]{0,2,3,1:T(8,128)(2,1)S(1)} %bitcast.185, bf16[512,5,3,64]{0,3,2,1:T(8,128)(2,1)S(1)} %bitcast.182, pred[512,1024]{0,1:T(8,128)(4,1)S(1)} %copy-done.7), kind=kOutput, calls=%fused_computation.119 | convolution fusion | flops 1030218240 | bytes 33650688 | tf_op jit(solution)/shard_map/qkrd,skd->krqs/dot_general | solution.py:71
  93.9 12.8 %fusion.3 = f32[5,3,512]{2,1,0:T(4,128)S(1)} fusion(f32[5,3,512,1024]{2,3,1,0:T(8,128)} %get-tuple-element.52, f32[5,3,512]{2,1,0:T(4,128)S(1)} %get-tuple-element.51), kind=kLoop, calls=%fused_computation.9 | loop fusion | flops 15720960 | bytes 31518720 | tf_op jit(solution)/shard_map/reduce_sum | solution.py:136
  106.7 13.8 %fusion.42 = bf16[5,64,3,512]{3,1,2,0:T(8,128)(2,1)} fusion(bf16[1024,5,64,1]{0,2,3,1:T(8,128)(2,1)S(1)} %bitcast.190, f32[5,3,512,1024]{2,3,1,0:T(8,128)} %get-tuple-element.52, f32[5,3,512]{2,1,0:T(4,128)S(1)} %fusion.3, f32[5,3,512]{2,1,0:T(4,128)S(1)} %get-tuple-element.51), kind=kOutput, calls=%fused_computation.73 | convolution fusion | flops 1030717440 | bytes 33157120 | tf_op jit(solution)/shard_map/nluh,hng->unlg/dot_general | solution.py:140
  126.9 33.6 %all-gather.10.cloned.1.call-done = bf16[1024,960]{0,1:T(8,128)(2,1)} async-done(((bf16[512,960]{0,1:T(8,128)(2,1)}), bf16[1024,960]{0,1:T(8,128)(2,1)}) %all-gather.10.cloned.1.call-update) | async-done | bytes 1966096 | tf_op jit(solution)/shard_map/all_gather | solution.py:149
  160.5 7.7 %fusion.73 = f32[1024,1280]{1,0:T(8,128)} fusion(bf16[1024,960]{0,1:T(8,128)(2,1)} %all-gather.10.cloned.1.call-done, bf16[1280,960]{0,1:T(8,128)(2,1)} %param.23), kind=kOutput, calls=%fused_computation.121 | convolution fusion | flops 2516582400 | bytes 9666560 | tf_op jit(solution)/shard_map/dot_general | solution.py:25
  168.1 4.8 fusion.72
  172.9 20.6 %all-gather.12.cloned.1.call-done = bf16[1,1024,960]{1,2,0:T(8,128)(2,1)} async-done(((bf16[1,512,960]{1,2,0:T(8,128)(2,1)}), bf16[1,1024,960]{1,2,0:T(8,128)(2,1)}) %all-gather.12.cloned.1.call-update) | async-done | bytes 1966096 | tf_op jit(solution)/shard_map/all_gather | solution.py:160
  193.5 9.9 %multiply_convert_fusion = (bf16[1024,1280]{1,0:T(8,128)(2,1)S(1)}, bf16[1024,1280]{1,0:T(8,128)(2,1)S(1)}, bf16[1024,1280]{1,0:T(8,128)(2,1)}) fusion(f32[1024,1280]{1,0:T(8,128)} %fusion.72, f32[1024,1280]{1,0:T(8,128)} %fusion.73, bf16[1280,960]{0,1:T(8,128)(2,1)S(1)} %copy-done, bf16[1,1024,960]{1,2,0:T(8,128)(2,1)} %all-gather.12.cloned.1.call-done), kind=kOutput, calls=%fused_computation.14 | convolution fusion | flops 2537553920 | bytes 22773760 | tf_op jit(solution)/shard_map/dot_general | solution.py:25
  206.9 3.9 add_convert_fusion
  210.9 5.7 convolution_convert_fusion.3
  217.1 24.3 %reduce-scatter.11.cloned.1.call-done = bf16[512,960]{0,1:T(8,128)(2,1)} async-done(((bf16[1024,960]{0,1:T(8,128)(2,1)}), bf16[512,960]{0,1:T(8,128)(2,1)}) %reduce-scatter.11.cloned.1.call-update) | async-done | bytes 983056 | tf_op jit(solution)/shard_map/reduce_scatter | solution.py:165
  243.4 31.1 %reduce-scatter.9.cloned.1.call-done = bf16[512,960]{0,1:T(8,128)(2,1)} async-done(((bf16[1024,960]{0,1:T(8,128)(2,1)}), bf16[512,960]{0,1:T(8,128)(2,1)}) %reduce-scatter.9.cloned.1.call-update) | async-done | bytes 983056 | tf_op jit(solution)/shard_map/reduce_scatter | solution.py:153
  279.4 13.5 %fusion.46 = bf16[5,64,1024]{2,1,0:T(8,128)(2,1)} fusion(bf16[512,5,3,64]{0,3,2,1:T(8,128)(2,1)S(1)} %bitcast.186, f32[5,3,512,1024]{2,3,1,0:T(8,128)} %get-tuple-element.52, f32[5,3,512]{2,1,0:T(4,128)S(1)} %log_add_fusion), kind=kOutput, calls=%fused_computation.78 | convolution fusion | flops 1022689280 | bytes 33126400 | tf_op jit(solution)/shard_map/krqs,qkrd->skd/dot_general | solution.py:196
  292.9 23.5 %fusion = (f32[5,3,512]{2,1,0:T(4,128)S(1)}, f32[5,1024,512,3]{2,1,3,0:T(8,128)}) fusion(f32[5,3,512,1024]{2,3,1,0:T(8,128)} %get-tuple-element.52, f32[5,3,512]{2,1,0:T(4,128)S(1)} %log_add_fusion, bf16[1024,5,64,1]{0,2,3,1:T(8,128)(2,1)S(1)} %bitcast.191, bf16[512,5,3,64]{0,3,2,1:T(8,128)(2,1)S(1)} %bitcast.187), kind=kOutput, calls=%fused_computation.2 | convolution fusion | flops 1030218240 | bytes 64614400 | tf_op jit(solution)/shard_map/qkrd,skd->krqs/dot_general | solution.py:190
  316.5 26.9 %fusion.2 = bf16[5,3,512,1024]{2,3,1,0:T(8,128)(2,1)} fusion(f32[5,1024,512,3]{2,1,3,0:T(8,128)} %get-tuple-element.56, f32[5,3,512,1024]{2,3,1,0:T(8,128)} %get-tuple-element.52, f32[5,3,512]{2,1,0:T(4,128)S(1)} %get-tuple-element.55, f32[5,3,512]{2,1,0:T(4,128)S(1)} %log_add_fusion), kind=kLoop, calls=%fused_computation.4 | loop fusion | flops 31457280 | bytes 78704640 | tf_op jit(solution)/shard_map/convert_element_type | solution.py:201
  343.4 11.1 %fusion.50 = bf16[5,64,1024]{2,1,0:T(8,128)(2,1)} fusion(bf16[512,5,3,64]{0,3,2,1:T(8,128)(2,1)S(1)} %bitcast.183, bf16[5,3,512,1024]{2,3,1,0:T(8,128)(2,1)} %fusion.2), kind=kOutput, calls=%fused_computation.80 | convolution fusion | flops 1007288320 | bytes 17367040 | tf_op jit(solution)/shard_map/krqs,qkrd->skd/dot_general | solution.py:213
  357.2 13.6 %reduce-scatter.13.cloned.1.call-done = bf16[512,320]{0,1:T(8,128)(2,1)} async-done(((bf16[1024,320]{0,1:T(8,128)(2,1)}), bf16[512,320]{0,1:T(8,128)(2,1)}) %reduce-scatter.13.cloned.1.call-update) | async-done | bytes 327696 | tf_op jit(solution)/shard_map/reduce_scatter | solution.py:219
  377.7 8.7 %fusion.75 = f32[5,64,3,512]{3,1,2,0:T(8,128)S(1)} fusion(bf16[1024,5,64,1]{0,2,3,1:T(8,128)(2,1)} %bitcast.184, bf16[5,3,512,1024]{2,3,1,0:T(8,128)(2,1)} %fusion.2), kind=kOutput, calls=%fused_computation.123 | convolution fusion | flops 1006632960 | bytes 18350080 | tf_op jit(solution)/shard_map/nluh,hng->unlg/dot_general | solution.py:207
  392.1 6.6 convolution_convert_fusion
  398.7 3.9 convolution_convert_fusion.1
  402.7 3.9 convolution_convert_fusion.2
  407.9 32.7 %reduce-scatter.23.cloned.1.call-done = bf16[480,960]{1,0:T(8,128)(2,1)} async-done(((bf16[960,960]{1,0:T(8,128)(2,1)}), bf16[480,960]{1,0:T(8,128)(2,1)}) %reduce-scatter.23.cloned.1.call-update) | async-done | bytes 921616 | tf_op jit(solution)/shard_map/reduce_scatter | solution.py:265
  440.5 33.2 %reduce-scatter.17.cloned.1.call-done = bf16[480,960]{1,0:T(8,128)(2,1)} async-done(((bf16[960,960]{1,0:T(8,128)(2,1)}), bf16[480,960]{1,0:T(8,128)(2,1)}) %reduce-scatter.17.cloned.1.call-update) | async-done | bytes 921616 | tf_op jit(solution)/shard_map/reduce_scatter | solution.py:247
  481.4 4.9 all-reduce.6
  486.5 33.8 %all-reduce.4 = (bf16[480]{0:T(512)(128)(2,1)S(1)}, bf16[480]{0:T(512)(128)(2,1)S(1)}) all-reduce(bf16[480]{0:T(512)(128)(2,1)S(1)} %dynamic-slice.4, bf16[480]{0:T(512)(128)(2,1)S(1)} %dynamic-slice.6), channel_id=1, replica_groups=mesh['fsdp'=2,'replica'=16] {'replica'}, use_global_device_ids=true, to_apply=%region_13.14 | all-reduce | flops 960 | bytes 3840 | tf_op jit(solution)/shard_map/psum | solution.py:280
  521.4 4.0 fusion.28
  525.4 150.1 %all-reduce.10.cloned.1.call-done = (bf16[480,960]{1,0:T(8,128)(2,1)}, bf16[160,960]{1,0:T(8,128)(2,1)}, bf16[160,960]{1,0:T(8,128)(2,1)}, bf16[480,960]{1,0:T(8...) async-done(((bf16[480,960]{1,0:T(8,128)(2,1)}, bf16[160,960]{1,0:T(8,128)(2,1)}, bf16[160,960]{1,0:T(8,128)(2,1)}, ...) | async-done | bytes 9830416 | tf_op jit(solution)/shard_map/psum | solution.py:276
  (194 shorter events, 69.8 us)
Async XLA Ops:
  7.2 186.3 %copy-start = (bf16[1280,960]{0,1:T(8,128)(2,1)S(1)}, bf16[1280,960]{0,1:T(8,128)(2,1)}, u32[]{:S(2)}) copy-start(bf16[1280,960]{0,1:T(8,128)(2,1)} %param.24) | copy-start | bytes 7372804
  7.2 69.0 %all-gather.6.cloned.1.call-start = ((), (), s32[]{:S(2)}) async-start(), calls=%async_computation.8 | async-start | bytes 2949120 | tf_op jit(solution)/shard_map/all_gather | solution.py:100
  8.0 112.6 %all-gather.8.cloned.1.call-start = ((), (), s32[]{:S(2)}) async-start(), calls=%async_computation.9 | async-start | bytes 2949120 | tf_op jit(solution)/shard_map/all_gather | solution.py:103
  8.7 151.7 %all-gather.10.cloned.1.call-start = ((), (), s32[]{:S(2)}) async-start(), calls=%async_computation.10 | async-start | bytes 2949120 | tf_op jit(solution)/shard_map/all_gather | solution.py:149
  9.1 67.1 %copy-start.34 = (f32[512]{0:T(512)}, f32[512]{0:T(512)S(1)}, u32[]{:S(2)}) copy-start(f32[512]{0:T(512)S(1)} %add_rsqrt_fusion.1) | copy-start | bytes 6148
  16.8 59.5 %copy-start.32 = (f32[960]{0:T(1024)}, f32[960]{0:T(1024)S(1)}, u32[]{:S(2)}) copy-start(f32[960]{0:T(1024)S(1)} %convert_element_type.209) | copy-start | bytes 11524
  33.5 17.6 %copy-start.15 = (bf16[320,960]{1,0:T(8,128)(2,1)}, bf16[320,960]{1,0:T(8,128)(2,1)S(1)}, u32[]{:S(2)}) copy-start(bf16[320,960]{1,0:T(8,128)(2,1)S(1)} %all_gather.33) | copy-start | bytes 1843204
  61.6 13.4 %copy-start.36 = (s32[1,1024]{1,0:T(1,128)S(1)}, s32[1,1024]{1,0:T(1,128)}, u32[]{:S(2)}) copy-start(s32[1,1024]{1,0:T(1,128)} %param.14) | copy-start | bytes 12292
  80.6 13.3 %copy-start.4 = (bf16[512,15,64]{0,2,1:T(8,128)(2,1)}, bf16[512,15,64]{0,2,1:T(8,128)(2,1)S(1)}, u32[]{:S(2)}) copy-start(bf16[512,15,64]{0,2,1:T(8,128)(2,1)S(1)} %fusion.34) | copy-start | bytes 2949124
  93.9 12.8 %copy-start.11 = (bf16[1024,320]{0,1:T(8,128)(2,1)S(1)}, bf16[1024,320]{0,1:T(8,128)(2,1)}, u32[]{:S(2)}) copy-start(bf16[1024,320]{0,1:T(8,128)(2,1)} %all_gather.32) | copy-start | bytes 1966084
  126.0 67.5 %all-gather.12.cloned.1.call-start = ((), (), s32[]{:S(2)}) async-start(), calls=%async_computation.19 | async-start | bytes 2949120 | tf_op jit(solution)/shard_map/all_gather | solution.py:160
  126.6 114.8 %reduce-scatter.11.cloned.1.call-start = ((), (), s32[]{:S(2)}) async-start(), calls=%async_computation.12 | async-start | bytes 2949120 | tf_op jit(solution)/shard_map/reduce_scatter | solution.py:165
  160.4 7.7 %copy-start.41 = (bf16[1280,960]{0,1:T(8,128)(2,1)S(1)}, bf16[1280,960]{0,1:T(8,128)(2,1)}, u32[]{:S(2)}) copy-start(bf16[1280,960]{0,1:T(8,128)(2,1)} %param.22) | copy-start | bytes 7372804
  160.5 7.7 %copy-start.46 = (bf16[1024,960]{0,1:T(8,128)(2,1)S(1)}, bf16[1024,960]{0,1:T(8,128)(2,1)}, u32[]{:S(2)}) copy-start(bf16[1024,960]{0,1:T(8,128)(2,1)} %all-gather.10.cloned.1.call-done) | copy-start | bytes 5898244
  193.5 9.9 %copy-start.42 = (bf16[1280,960]{0,1:T(8,128)(2,1)S(1)}, bf16[1280,960]{0,1:T(8,128)(2,1)}, u32[]{:S(2)}) copy-start(bf16[1280,960]{0,1:T(8,128)(2,1)} %param.22) | copy-start | bytes 7372804
  210.9 63.7 %reduce-scatter.9.cloned.1.call-start = ((), (), s32[]{:S(2)}) async-start(), calls=%async_computation.11 | async-start | bytes 2949120 | tf_op jit(solution)/shard_map/reduce_scatter | solution.py:153
  216.6 24.8 %copy-start.3 = (f32[512,960]{0,1:T(8,128)S(1)}, f32[512,960]{0,1:T(8,128)}, u32[]{:S(2)}) copy-start(f32[512,960]{0,1:T(8,128)} %copy-done.2) | copy-start | bytes 5898244
  216.6 138.0 %reduce-scatter.15.cloned.1.call-start = ((), (), s32[]{:S(2)}) async-start(), calls=%async_computation.14 | async-start | bytes 983040 | tf_op jit(solution)/shard_map/reduce_scatter | solution.py:222
  279.4 13.5 %copy-start.12 = (bf16[1024,320]{0,1:T(8,128)(2,1)S(1)}, bf16[1024,320]{0,1:T(8,128)(2,1)}, u32[]{:S(2)}) copy-start(bf16[1024,320]{0,1:T(8,128)(2,1)} %all_gather.32) | copy-start | bytes 1966084
  316.5 54.3 %reduce-scatter.13.cloned.1.call-start = ((), (), s32[]{:S(2)}) async-start(), calls=%async_computation.13 | async-start | bytes 983040 | tf_op jit(solution)/shard_map/reduce_scatter | solution.py:219
  316.5 26.9 %copy-start.5 = (bf16[512,15,64]{0,2,1:T(8,128)(2,1)S(1)}, bf16[512,15,64]{0,2,1:T(8,128)(2,1)}, u32[]{:S(2)}) copy-start(bf16[512,15,64]{0,2,1:T(8,128)(2,1)} %copy-done.4) | copy-start | bytes 2949124
  343.4 11.2 %copy-start.33 = (f32[960]{0:T(1024)S(1)}, f32[960]{0:T(1024)}, u32[]{:S(2)}) copy-start(f32[960]{0:T(1024)} %copy-done.32) | copy-start | bytes 11524
  343.4 11.2 %copy-start.35 = (f32[512]{0:T(512)S(1)}, f32[512]{0:T(512)}, u32[]{:S(2)}) copy-start(f32[512]{0:T(512)} %copy-done.34) | copy-start | bytes 6148
  354.6 16.3 %copy-start.22 = (f32[512,64]{0,1:T(8,128)S(1)}, f32[512,64]{0,1:T(8,128)}, u32[]{:S(2)}) copy-start(f32[512,64]{0,1:T(8,128)} %copy-done.20) | copy-start | bytes 393220
  354.6 52.0 %reduce-scatter.21.cloned.1.call-start = ((), (), s32[]{:S(2)}) async-start(), calls=%async_computation.17 | async-start | bytes 983040 | tf_op jit(solution)/shard_map/reduce_scatter | solution.py:259
  357.2 14.9 %copy-start.25 = (f32[512,64]{0,1:T(8,128)S(1)}, f32[512,64]{0,1:T(8,128)}, u32[]{:S(2)}) copy-start(f32[512,64]{0,1:T(8,128)} %copy-done.23) | copy-start | bytes 393220
  357.2 50.7 %reduce-scatter.19.cloned.1.call-start = ((), (), s32[]{:S(2)}) async-start(), calls=%async_computation.16 | async-start | bytes 983040 | tf_op jit(solution)/shard_map/reduce_scatter | solution.py:253
  373.7 66.8 %reduce-scatter.23.cloned.1.call-start = ((), (), s32[]{:S(2)}) async-start(), calls=%async_computation.18 | async-start | bytes 2949120 | tf_op jit(solution)/shard_map/reduce_scatter | solution.py:265
  377.7 8.8 %copy-start.30 = (f32[512,64]{0,1:T(8,128)S(1)}, f32[512,64]{0,1:T(8,128)}, u32[]{:S(2)}) copy-start(f32[512,64]{0,1:T(8,128)} %get-tuple-element.45) | copy-start | bytes 393220
  377.7 96.0 %reduce-scatter.17.cloned.1.call-start = ((), (), s32[]{:S(2)}) async-start(), calls=%async_computation.15 | async-start | bytes 2949120 | tf_op jit(solution)/shard_map/reduce_scatter | solution.py:247
  392.0 283.4 %all-reduce.10.cloned.1.call-start = ((), (), s32[]{:S(2)}) async-start(), calls=%async_computation.20 | async-start | bytes 19988480 | tf_op jit(solution)/shard_map/psum | solution.py:276
  392.0 6.7 copy-start.47
  (33 other events, 71.2 us)
Sparse Core Ops, SparseCore 0:
  9.6 48.1 all-gather.5
  59.3 33.5 all-gather.7
  126.2 34.2 all-gather.9
  161.8 31.6 all-gather.11
  211.0 30.3 reduce-scatter.10
  244.2 30.3 reduce-scatter.8
  316.6 15.9 reduce-scatter.14
  354.7 16.0 reduce-scatter.12
  373.1 15.9 reduce-scatter.20
  391.8 15.9 reduce-scatter.18
  410.1 30.3 reduce-scatter.22
  443.3 30.3 reduce-scatter.16
  479.1 196.3 all-reduce.9
where the time goes:
time: 701 us; the launch traced here: 698 us
  waiting for transfers between devices  343 us (49%)
  matrix products  155 us (22%)
  blocking collectives  99.5 us (14%)
  other arithmetic  75.8 us (11%)
  between operations  16 us (2%)
  local copies, waits for them, and re-layouts  7.47 us (1%)
    psum x1, waiting for transfers between devices, on_device(): lax.psum(query_sum.astype(jnp.bfloat16), 'replica').astype(jnp.float32)  150 us
    psum x1, blocking collectives, on_device(): lax.psum(gain_first_sum.astype(jnp.bfloat16), 'replica').astype(jnp.float32)  33.8 us
    all_gather x1, waiting for transfers between devices, on_device(): every_hidden = lax.all_gather(hidden_two, 'fsdp', axis=0, tiled=True)  33.6 us
    reduce_scatter x1, waiting for transfers between devices, on_device(): lax.psum_scatter(contract_rows(query_back, hidden_state).astype(jnp.bfloa...  33.2 us
    reduce_scatter x1, waiting for transfers between devices, on_device(): lax.psum_scatter(out_term.astype(jnp.bfloat16), 'fsdp', scatter_dimension...  32.7 us
    reduce_scatter x1, waiting for transfers between devices, on_device(): lax.psum_scatter(jnp.dot(active, down_weight, preferred_element_type=jnp....  31.1 us
    dot_general x7, matrix products, project_rows(): lax.dot_general(left, weight, (((1,), (1,)), ((), ())), preferred_element...  29.3 us
    convert_element_type x1, other arithmetic, on_device(): score_back = (attend_full * (attend_back - jnp.sum(attend_full * attend_b...  26.9 us
  transfers between devices with their start and end apart: 13, of which 9 were waited for; matrix products, arithmetic and copies ran while one was open for 22% of the time, Pallas kernels for 0%

commit v1 on v0

v1 whole, which is shorter than its diff:
```python
import functools

import jax
import jax.numpy as jnp
from jax import lax
from jax.experimental import pallas as pl
from jax.experimental.pallas import tpu as pltpu
from jax.sharding import PartitionSpec as P

QUERY_HEADS = 15
KEY_VALUE_HEADS = 5
HEAD_SIZE = 64


norm_eps = 1e-05
rotary_base = 100000.0


def normalize_parts(value_rows):
    factor = lax.rsqrt(jnp.mean(value_rows * value_rows, axis=-1, keepdims=True) + norm_eps)
    return (value_rows * factor, factor)


def norm_back(upstream, normed, factor):
    return factor * (upstream - normed * jnp.mean(upstream * normed, axis=-1, keepdims=True))


def project_rows(left, weight):
    return lax.dot_general(
        left, weight, (((1,), (1,)), ((), ())), preferred_element_type=jnp.float32
    )


def contract_rows(left, right):
    return lax.dot_general(
        left, right, (((0,), (0,)), ((), ())), preferred_element_type=jnp.float32
    )


def swiglu_back(active_back, gate, up):
    sigma = jax.nn.sigmoid(gate)
    gate_back = (active_back * up * sigma * (1.0 + gate * (1.0 - sigma))).astype(jnp.bfloat16)
    up_back = (active_back * gate * sigma).astype(jnp.bfloat16)
    return (gate_back, up_back)


def dims(left, right, left_axis, right_axis):
    return lax.dot_general(
        left, right, (((left_axis,), (right_axis,)), ((), ())), preferred_element_type=jnp.float32
    )


def rotary_tables(positions):
    half = HEAD_SIZE // 2
    frequency = rotary_base ** (-(jnp.arange(half, dtype=jnp.float32) * 2.0 / HEAD_SIZE))
    angles = frequency[:, None] * positions.astype(jnp.float32)[None, :]
    cosine, sine = jnp.cos(angles), jnp.sin(angles)
    return (
        jnp.concatenate([cosine, cosine], axis=0)[None],
        jnp.concatenate([sine, sine], axis=0)[None],
    )


def apply_rotary(field, cosine_table, sine_table):
    half = HEAD_SIZE // 2
    turned = jnp.concatenate([-field[:, half:], field[:, :half]], axis=1)
    return field * cosine_table + turned * sine_table


def apply_rotary_back(field, cosine_table, sine_table):
    half = HEAD_SIZE // 2
    scaled = field * sine_table
    turned = jnp.concatenate([scaled[:, half:], -scaled[:, :half]], axis=1)
    return field * cosine_table + turned


def fill_bias(me_ref, segk_ref, segq_ref, bias_ref):
    @pl.when(pl.program_id(0) == 0)
    def _():
        keys, queries = bias_ref.shape
        key_index = lax.broadcasted_iota(jnp.int32, (keys, queries), 0)
        query_index = lax.broadcasted_iota(jnp.int32, (keys, queries), 1) + me_ref[0] * queries
        allowed = (segk_ref[...] == segq_ref[...]) & (key_index <= query_index)
        bias_ref[...] = jnp.where(allowed, 0.0, -1e30)


def attend_kernel(
    parts, block, me_ref, segk_ref, segq_ref, q_ref, k_ref, v_ref, o_ref, lse_ref, bias_ref
):
    fill_bias(me_ref, segk_ref, segq_ref, bias_ref)
    group, _, tokens = q_ref.shape

    for part in range(parts):

        @pl.when(me_ref[0] == part)
        def _():
            for start in range(0, tokens, block):
                span = part * tokens + start + block
                for head in range(group):
                    columns = slice(start, start + block)
                    scores = dims(k_ref[0, :, :span], q_ref[head, :, columns], 0, 0)
                    scores = scores + bias_ref[:span, columns]
                    top = jnp.max(scores, axis=0, keepdims=True)
                    raised = jnp.exp(scores - top)
                    total = jnp.sum(raised, axis=0, keepdims=True)
                    mixed = dims(v_ref[0, :, :span], raised.astype(jnp.bfloat16), 1, 0)
                    o_ref[head, :, columns] = (mixed / total).astype(jnp.bfloat16)
                    lse_ref[head, :, columns] = top + jnp.log(total)


def attend_back_kernel(
    parts,
    block,
    me_ref,
    segk_ref,
    segq_ref,
    q_ref,
    k_ref,
    v_ref,
    o_ref,
    lse_ref,
    do_ref,
    dq_ref,
    dk_ref,
    dv_ref,
    bias_ref,
):
    fill_bias(me_ref, segk_ref, segq_ref, bias_ref)
    group, _, tokens = q_ref.shape
    dk_ref[...] = jnp.zeros_like(dk_ref)
    dv_ref[...] = jnp.zeros_like(dv_ref)

    for part in range(parts):

        @pl.when(me_ref[0] == part)
        def _():
            for start in range(0, tokens, block):
                span = part * tokens + start + block
                for head in range(group):
                    columns = slice(start, start + block)
                    query = q_ref[head, :, columns]
                    back = do_ref[head, :, columns]
                    delta = jnp.sum(
                        back.astype(jnp.float32) * o_ref[head, :, columns].astype(jnp.float32),
                        axis=0,
                        keepdims=True,
                    )
                    scores = dims(k_ref[0, :, :span], query, 0, 0) + bias_ref[:span, columns]
                    attend = jnp.exp(scores - lse_ref[head, :, columns])
                    attend_back = dims(v_ref[0, :, :span], back, 0, 0)
                    score_back = (attend * (attend_back - delta)).astype(jnp.bfloat16)
                    dv_ref[0, :, :span] += dims(back, attend.astype(jnp.bfloat16), 1, 1)
                    dk_ref[0, :, :span] += dims(query, score_back, 1, 1)
                    dq_ref[head, :, columns] = dims(k_ref[0, :, :span], score_back, 1, 0)


def attention_specs(tokens, sequence):
    group = QUERY_HEADS // KEY_VALUE_HEADS
    return dict(
        me=pl.BlockSpec(memory_space=pltpu.SMEM),
        segk=pl.BlockSpec((sequence, 1), lambda h: (0, 0)),
        segq=pl.BlockSpec((1, tokens), lambda h: (0, 0)),
        query=pl.BlockSpec((group, HEAD_SIZE, tokens), lambda h: (h, 0, 0)),
        key=pl.BlockSpec((1, HEAD_SIZE, sequence), lambda h: (h, 0, 0)),
        row=pl.BlockSpec((group, 1, tokens), lambda h: (h, 0, 0)),
    )


def attend(parts, me, segk, segq, query, key, value):
    tokens, sequence = query.shape[2], key.shape[2]
    sp = attention_specs(tokens, sequence)
    pairs = QUERY_HEADS * tokens * sequence
    return pl.pallas_call(
        functools.partial(attend_kernel, parts, min(tokens, 256)),
        grid=(KEY_VALUE_HEADS,),
        in_specs=[sp["me"], sp["segk"], sp["segq"], sp["query"], sp["key"], sp["key"]],
        out_specs=[sp["query"], sp["row"]],
        out_shape=[
            jax.ShapeDtypeStruct(query.shape, jnp.bfloat16),
            jax.ShapeDtypeStruct((QUERY_HEADS, 1, tokens), jnp.float32),
        ],
        scratch_shapes=[pltpu.VMEM((sequence, tokens), jnp.float32)],
        compiler_params=pltpu.CompilerParams(vmem_limit_bytes=40 * 2**20),
        cost_estimate=pl.CostEstimate(
            flops=16 * HEAD_SIZE * pairs, bytes_accessed=4 * 2**20, transcendentals=pairs
        ),
    )(me, segk, segq, query, key, value)


def attend_grads(parts, me, segk, segq, query, key, value, mixed, lse, back):
    tokens, sequence = query.shape[2], key.shape[2]
    sp = attention_specs(tokens, sequence)
    pairs = QUERY_HEADS * tokens * sequence
    return pl.pallas_call(
        functools.partial(attend_back_kernel, parts, min(tokens, 256)),
        grid=(KEY_VALUE_HEADS,),
        in_specs=[sp["me"], sp["segk"], sp["segq"], sp["query"], sp["key"], sp["key"]]
        + [sp["query"], sp["row"], sp["query"]],
        out_specs=[sp["query"], sp["key"], sp["key"]],
        out_shape=[
            jax.ShapeDtypeStruct(query.shape, jnp.float32),
            jax.ShapeDtypeStruct(key.shape, jnp.float32),
            jax.ShapeDtypeStruct(key.shape, jnp.float32),
        ],
        scratch_shapes=[pltpu.VMEM((sequence, tokens), jnp.float32)],
        compiler_params=pltpu.CompilerParams(vmem_limit_bytes=48 * 2**20),
        cost_estimate=pl.CostEstimate(
            flops=40 * HEAD_SIZE * pairs, bytes_accessed=10 * 2**20, transcendentals=pairs
        ),
    )(me, segk, segq, query, key, value, mixed, lse, back)


def swap(block, axis, size, bit=0):
    return lax.ppermute(block, axis, [(i, i ^ (1 << bit)) for i in range(size)])


def place(mine, other, which):
    rows = mine.shape[0]
    both = jnp.zeros((2 * rows,) + mine.shape[1:], mine.dtype)
    both = lax.dynamic_update_slice_in_dim(both, mine, which * rows, 0)
    return lax.dynamic_update_slice_in_dim(both, other, (1 - which) * rows, 0)


def take(block, which):
    rows = block.shape[0] // 2
    return lax.dynamic_slice_in_dim(block, which * rows, rows)


def halve(block, axis, size, bit=0):
    which = (lax.axis_index(axis) >> bit) & 1
    return take(block, which) + swap(take(block, 1 - which), axis, size, bit)


def unhalve(block, axis, size, bit=0):
    which = (lax.axis_index(axis) >> bit) & 1
    return place(block, swap(block, axis, size, bit), which)


def gather_weight(weight, fsdp, replica):
    if fsdp != 2 or replica % 2 or weight.ndim == 1:
        return lax.all_gather(weight, "fsdp", axis=0, tiled=True)
    part = swap(take(weight, lax.axis_index("replica") & 1), "fsdp", fsdp)
    other = unhalve(part, "replica", replica)
    return place(weight, other, lax.axis_index("fsdp"))


def scatter_rows(block, fsdp):
    if fsdp != 2:
        return lax.psum_scatter(block, "fsdp", scatter_dimension=0, tiled=True)
    return halve(block, "fsdp", fsdp)


def replica_sum(block, replica):
    bits = replica.bit_length() - 1
    rows = block.shape[0]
    if replica != 1 << bits or rows % (2 * replica) or bits < 2:
        return lax.psum(block, "replica")
    block = halve(block, "replica", replica, 0)
    rows = block.shape[0] // 2
    orders = [list(range(1, bits)), list(range(1, bits))[::-1]]
    pieces = [block[:rows], block[rows:]]
    for step in range(bits - 1):
        pieces = [halve(p, "replica", replica, o[step]) for p, o in zip(pieces, orders)]
    for step in reversed(range(bits - 1)):
        pieces = [unhalve(p, "replica", replica, o[step]) for p, o in zip(pieces, orders)]
    return unhalve(jnp.concatenate(pieces), "replica", replica, 0)


def feed_forward(hidden, back, gate_weight, up_weight, down_weight):
    gate = project_rows(hidden, gate_weight)
    up = project_rows(hidden, up_weight)
    active = (gate * jax.nn.sigmoid(gate) * up).astype(jnp.bfloat16)
    gate_back, up_back = swiglu_back(project_rows(back, down_weight), gate, up)
    hidden_back = (
        jnp.dot(gate_back, gate_weight, preferred_element_type=jnp.float32)
        + jnp.dot(up_back, up_weight, preferred_element_type=jnp.float32)
    ).astype(jnp.bfloat16)
    down = jnp.dot(active, down_weight, preferred_element_type=jnp.float32).astype(jnp.bfloat16)
    return hidden_back, down, active, gate_back, up_back


def on_device(
    fsdp,
    replica,
    inputs,
    segment_ids,
    positions,
    attn_gain,
    q_weight,
    key_matrix,
    value_matrix,
    o_weight,
    ffn_gain,
    gate_weight,
    up_weight,
    down_weight,
    cotangent,
):
    tokens = inputs.shape[1]
    scale = HEAD_SIZE ** (-0.5)
    me = lax.axis_index("fsdp")
    me_ref = me.astype(jnp.int32)[None]
    data = inputs[0].astype(jnp.float32)
    segments = segment_ids[0]
    segk = segments[:, None]
    segq = lax.dynamic_slice_in_dim(segments, me * tokens, tokens)[None]
    cosine_table, sine_table = rotary_tables(positions[0])
    down_back = cotangent[0]
    back_out = down_back.astype(jnp.float32)

    kv_weight = jnp.concatenate([key_matrix, value_matrix])
    kv_rows = key_matrix.shape[0]
    gains = jnp.stack([attn_gain, ffn_gain], axis=1)
    gains = lax.all_gather(gains, "fsdp", axis=0, tiled=True) if fsdp != 2 else place(
        gains, swap(gains, "fsdp", fsdp), me
    )
    gain_first = gains[:, 0].astype(jnp.float32)
    gain_second = gains[:, 1].astype(jnp.float32)
    kv_gathered = gather_weight(kv_weight, fsdp, replica).reshape(fsdp, 2, kv_rows, -1)
    kv_full = jnp.swapaxes(kv_gathered, 0, 1).reshape(2 * fsdp * kv_rows, -1)
    q_weight, kv_full = lax.optimization_barrier((q_weight, kv_full))
    query_full = gather_weight(q_weight, fsdp, replica)

    normed, factor_one = normalize_parts(data)
    hidden_state = (normed * gain_first).astype(jnp.bfloat16)
    kv_lin = project_rows(kv_full, hidden_state).reshape(2 * KEY_VALUE_HEADS, HEAD_SIZE, tokens)
    kv_own = jnp.concatenate(
        [
            apply_rotary(kv_lin[:KEY_VALUE_HEADS], cosine_table, sine_table),
            kv_lin[KEY_VALUE_HEADS:],
        ]
    ).astype(jnp.bfloat16)
    if fsdp == 2:
        kv_first = lax.ppermute(kv_own, "fsdp", [(0, 1)])
        kv_all = jnp.concatenate([jnp.where(me == 0, kv_own, kv_first), kv_own], axis=2)
    else:
        kv_all = lax.all_gather(kv_own, "fsdp", axis=2, tiled=True)
    keys, values = kv_all[:KEY_VALUE_HEADS], kv_all[KEY_VALUE_HEADS:]
    o_weight, down_back_sent, kv_own = lax.optimization_barrier((o_weight, down_back, kv_own))
    out_full = gather_weight(o_weight, fsdp, replica)
    if fsdp == 2:
        back_other = swap(down_back_sent, "fsdp", fsdp)
    queries = (
        apply_rotary(
            project_rows(query_full, hidden_state).reshape(QUERY_HEADS, HEAD_SIZE, tokens),
            cosine_table,
            sine_table,
        ).astype(jnp.bfloat16)
        * scale
    ).astype(jnp.bfloat16)
    mixed, lse = attend(fsdp, me_ref, segk, segq, queries, keys, values)
    mixed_rows = mixed.reshape(QUERY_HEADS * HEAD_SIZE, tokens)
    middle = data + dims(mixed_rows, out_full, 0, 1)
    normed_two, factor_two = normalize_parts(middle)
    hidden_two = (normed_two * gain_second).astype(jnp.bfloat16)

    weights = (gate_weight, up_weight, down_weight)
    if fsdp == 2:
        hidden_other = swap(hidden_two, "fsdp", fsdp)
        own = feed_forward(hidden_two, down_back, *weights)
        hidden_other, own = lax.optimization_barrier((hidden_other, own))
        other = feed_forward(hidden_other, back_other, *weights)
        came_back = swap(other[0], "fsdp", fsdp)
        came_down = swap(other[1], "fsdp", fsdp)
        hidden_two_back = own[0].astype(jnp.float32) + came_back.astype(jnp.float32)
        down = own[1].astype(jnp.float32) + came_down.astype(jnp.float32)
        halves = ((own, hidden_two, down_back), (other, hidden_other, back_other))
        ffn_terms = (
            sum(contract_rows(w[3], h) for w, h, b in halves),
            sum(contract_rows(w[4], h) for w, h, b in halves),
            sum(contract_rows(w[2], b) for w, h, b in halves),
        )
    else:
        every_hidden = lax.all_gather(hidden_two, "fsdp", axis=0, tiled=True)
        every_back = lax.all_gather(down_back, "fsdp", axis=0, tiled=True)
        work = feed_forward(every_hidden, every_back, *weights)
        hidden_two_back = scatter_rows(work[0], fsdp).astype(jnp.float32)
        down = scatter_rows(work[1], fsdp).astype(jnp.float32)
        ffn_terms = (
            contract_rows(work[3], every_hidden),
            contract_rows(work[4], every_hidden),
            contract_rows(work[2], every_back),
        )
    outputs = (middle + down).astype(jnp.bfloat16)[None]
    ffn_sums = [lax.psum(t.astype(jnp.bfloat16), "replica").astype(jnp.float32) for t in ffn_terms]

    gain_second_term = jnp.sum(hidden_two_back * normed_two, axis=0)
    middle_back = back_out + norm_back(hidden_two_back * gain_second, normed_two, factor_two)
    attn_back = middle_back.astype(jnp.bfloat16)
    mixed_back = dims(out_full, attn_back, 0, 1).astype(jnp.bfloat16)
    out_term = dims(attn_back, mixed_rows, 0, 1).astype(jnp.bfloat16)
    query_rot_back, key_term, value_term = attend_grads(
        fsdp,
        me_ref,
        segk,
        segq,
        queries,
        keys,
        values,
        mixed,
        lse,
        mixed_back.reshape(mixed.shape),
    )
    kv_term = jnp.concatenate([key_term, value_term])
    if fsdp == 2:
        kv_sent = lax.ppermute(kv_term[:, :, :tokens].astype(jnp.bfloat16), "fsdp", [(1, 0)])
        kv_back = jnp.where(
            me == 0,
            kv_term[:, :, :tokens] + kv_sent.astype(jnp.float32),
            kv_term[:, :, tokens:],
        )
    else:
        kv_back = lax.psum_scatter(
            kv_term.astype(jnp.bfloat16), "fsdp", scatter_dimension=2, tiled=True
        ).astype(jnp.float32)
    query_back = (
        apply_rotary_back(query_rot_back * scale, cosine_table, sine_table)
        .reshape(QUERY_HEADS * HEAD_SIZE, tokens)
        .astype(jnp.bfloat16)
    )
    kv_back = jnp.concatenate(
        [
            apply_rotary_back(kv_back[:KEY_VALUE_HEADS], cosine_table, sine_table),
            kv_back[KEY_VALUE_HEADS:],
        ]
    )
    kv_back = kv_back.reshape(2 * KEY_VALUE_HEADS * HEAD_SIZE, tokens).astype(jnp.bfloat16)
    hidden_back = dims(query_back, query_full, 0, 0) + dims(kv_back, kv_full, 0, 0)
    gain_first_term = jnp.sum(hidden_back * normed, axis=0)
    input_back = middle_back + norm_back(hidden_back * gain_first, normed, factor_one)

    def by_owner(term):
        return term.astype(jnp.bfloat16).reshape(fsdp, -1, term.shape[-1])

    kv_grad = jnp.dot(kv_back, hidden_state, preferred_element_type=jnp.float32)
    key_grad, value_grad = jnp.split(kv_grad, 2)
    query_grad = jnp.dot(query_back, hidden_state, preferred_element_type=jnp.float32)
    width = hidden_state.shape[-1]
    gain_terms = jnp.stack([gain_first_term, gain_second_term]).reshape(2, fsdp, -1)
    gain_terms = jnp.swapaxes(gain_terms, 0, 1).reshape(fsdp, -1)
    q_rows = q_weight.shape[0]
    pieces = [by_owner(t) for t in (query_grad, key_grad, value_grad, out_term)]
    used = sum(p.shape[1] for p in pieces)
    extra = -(used + 1) % (2 * replica * 2) + 1
    gain_rows = jnp.zeros((fsdp, extra, width), jnp.bfloat16)
    gain_rows = gain_rows.at[:, 0, : gain_terms.shape[1]].set(gain_terms.astype(jnp.bfloat16))
    late = jnp.concatenate(pieces + [gain_rows], axis=1)
    late = scatter_rows(late.reshape(-1, width), fsdp)
    late = replica_sum(late, replica).astype(jnp.float32)
    ends = [q_rows, q_rows + kv_rows, q_rows + 2 * kv_rows, 2 * q_rows + 2 * kv_rows]
    query_sum, key_sum, value_sum, out_sum, rest = jnp.split(late, ends)
    gain_len = attn_gain.shape[0]
    return (
        outputs,
        input_back[None],
        rest[0, :gain_len],
        query_sum,
        key_sum,
        value_sum,
        out_sum,
        rest[0, gain_len : 2 * gain_len],
        *ffn_sums,
    )


def solution(mesh):
    in_specs = (
        P("replica", "fsdp", None),
        P("replica", None),
        P("replica", "fsdp"),
        P("fsdp"),
        P("fsdp", None),
        P("fsdp", None),
        P("fsdp", None),
        P("fsdp", None),
        P("fsdp"),
        P("fsdp", None),
        P("fsdp", None),
        P("fsdp", None),
        P("replica", "fsdp", None),
    )
    out_specs = (
        P("replica", "fsdp", None),
        P("replica", "fsdp", None),
        P("fsdp"),
        P("fsdp", None),
        P("fsdp", None),
        P("fsdp", None),
        P("fsdp", None),
        P("fsdp"),
        P("fsdp", None),
        P("fsdp", None),
        P("fsdp", None),
    )
    return jax.shard_map(
        functools.partial(on_device, mesh.shape["fsdp"], mesh.shape["replica"]),
        mesh=mesh, in_specs=in_specs, out_specs=out_specs, check_vma=False
    )
```

time: 701 us -> 573 us (0.82)
  blocking collectives: 99.5 us -> 0 us
  matrix products: 155 us -> 65.6 us
  local copies, waits for them, and re-layouts: 7.47 us -> 84.9 us
  starting transfers between devices: 1.28 us -> 43.9 us
  waiting for transfers between devices: 343 us -> 301 us
  other arithmetic: 75.8 us -> 35 us
  Pallas kernels: 0 us -> 22.3 us
    ppermute x0 -> x28, waiting for transfers between devices: none -> 231 us  [the longest x26 218 us: swap(): return lax.ppermute(block, axis, [(i, i ^ 1 << bit) for i in range(size)])]
    reduce_scatter x8 -> x0, waiting for transfers between devices: 136 us -> none  [the longest x1 33.2 us: on_device(): lax.psum_scatter(contract_rows(query_back, hidden_state).astype(jnp.bfloa...]
    psum x1, waiting for transfers between devices: 150 us -> 70.3 us  [on_device(): lax.psum(t.astype(jnp.bfloat16), 'replica').astype(jnp.float32)]
    dot_general x13, matrix products: 101 us -> 24.9 us  [the longest x5 8.76 us: dims(): lax.dot_general(left, right, (((left_axis,), (right_axis,)), ((), ())), p...]
    all_gather x4 -> x0, blocking collectives: 54.9 us -> none  [the longest x1 17 us: on_device(): lax.all_gather(value_matrix, 'fsdp', axis=0, tiled=True)]
    all_gather x4 -> x0, waiting for transfers between devices: 54.2 us -> none  [the longest x1 33.6 us: on_device(): every_hidden = lax.all_gather(hidden_two, 'fsdp', axis=0, tiled=True)]
    ppermute x0 -> x28, starting transfers between devices: none -> 43.9 us  [the longest x26 37.6 us: swap(): return lax.ppermute(block, axis, [(i, i ^ 1 << bit) for i in range(size)])]
    convert_element_type x18 -> x8, other arithmetic: 47.6 us -> 10.3 us  [the longest x3 9.68 us: on_device(): lax.psum(t.astype(jnp.bfloat16), 'replica').astype(jnp.float32)]
  transfers between devices with their start and end apart: 13 -> 29, of which waited for: 9 -> 18; matrix products, arithmetic and copies ran while one was open for 22% -> 18% of each run, Pallas kernels for 0% -> 2%
where the time goes in v1:
time: 573 us; the launch traced here: 569 us
  waiting for transfers between devices  301 us (53%)
  local copies, waits for them, and re-layouts  84.9 us (15%)
  matrix products  65.6 us (11%)
  starting transfers between devices  43.9 us (8%)
  other arithmetic  35 us (6%)
  Pallas kernels  22.3 us (4%)
  between operations  15.7 us (3%)
    ppermute x26, waiting for transfers between devices, swap(): return lax.ppermute(block, axis, [(i, i ^ 1 << bit) for i in range(size)])  218 us
    psum x1, waiting for transfers between devices, on_device(): lax.psum(t.astype(jnp.bfloat16), 'replica').astype(jnp.float32)  70.3 us
    ppermute x26, starting transfers between devices, swap(): return lax.ppermute(block, axis, [(i, i ^ 1 << bit) for i in range(size)])  37.6 us
    unnamed x170, local copies, waits for them, and re-layouts  33.9 us
    dot_general x6, matrix products, contract_rows(): lax.dot_general(left, right, (((0,), (0,)), ((), ())), preferred_element_...  24.2 us
    dot_general x8, matrix products, project_rows(): lax.dot_general(left, weight, (((1,), (1,)), ((), ())), preferred_element...  16.4 us
    ppermute x1, waiting for transfers between devices, on_device(): lax.ppermute(kv_term[:, :, :tokens].astype(jnp.bfloat16), 'fsdp', [(1, 0)])  12.4 us
    dynamic_slice x12, local copies, waits for them, and re-layouts, take(): return lax.dynamic_slice_in_dim(block, which * rows, rows)  12.3 us
  transfers between devices with their start and end apart: 29, of which 18 were waited for; matrix products, arithmetic and copies ran while one was open for 18% of the time, Pallas kernels for 2%

profile of v1, /device:TPU:0, one launch (start us, length us, event | category | flops | bytes accessed | tf_op | source)
XLA Modules:
  0.0 568.5 jit_solution(9109612583900490266)
XLA Ops:
  31.2 4.7 collective-permute-start.5
  39.6 4.3 fusion.36
  47.4 13.3 %collective-permute-done.6 = bf16[240,960]{1,0:T(8,128)(2,1)} collective-permute-done((bf16[240,960]{1,0:T(8,128)(2,1)}, bf16[240,960]{1,0:T(8,128)(2,1)}, u32[]{:S(2)}, u32[]{:S(2)}) %collective-permute-start.6) | collective-permute-done | bytes 460832 | tf_op jit(solution)/shard_map/ppermute | solution.py:214
  60.8 10.5 %collective-permute-done.2 = bf16[240,960]{1,0:T(8,128)(2,1)} collective-permute-done((bf16[240,960]{1,0:T(8,128)(2,1)}, bf16[240,960]{1,0:T(8,128)(2,1)}, u32[]{:S(2)}, u32[]{:S(2)}) %collective-permute-start.2) | collective-permute-done | bytes 460832 | tf_op jit(solution)/shard_map/ppermute | solution.py:214
  79.5 10.6 %shard_map.212 = (bf16[15,64,512]{2,1,0:T(8,128)(2,1)S(1)}, f32[15,1,512]{2,1,0:T(1,128)S(1)}) custom-call(s32[1]{0:T(128)} %bitcast.1.me_ref, s32[1024,1]{1,0:T(8,128)S(1)} %copy-done.6, s32[1,512]{1,0:T(1,128)S(1)} %constant_dynamic-slice_fusion.12.segq_ref, bf16[15,64,512]{2,1,0:T(8,128)(2,1)S(1)} %fusion.22.q_ref, ...), custom_call_target="tpu_custom_call" | custom-call | flops 8053063680 | bytes 4194304 | tf_op jit(solution)/shard_map/pallas_call | solution.py:173
  91.7 13.1 %collective-permute-start.8 = (bf16[512,960]{0,1:T(8,128)(2,1)S(1)}, bf16[512,960]{0,1:T(8,128)(2,1)S(1)}, u32[]{:S(2)}, u32[]{:S(2)}) collective-permute-start(bf16[512,960]{0,1:T(8,128)(2,1)S(1)} %multiply_convert_fusion.6), channel_id=1, source_target_pairs={{0,16},{16,0},{1,17},{17,1},{2,18},{18,2},{3,19},{19,3},{4,20},{20... | collective-permute-start | bytes 2949128 | tf_op jit(solution)/shard_map/ppermute | solution.py:214
  115.3 11.9 %collective-permute-done.8 = bf16[512,960]{0,1:T(8,128)(2,1)S(1)} collective-permute-done((bf16[512,960]{0,1:T(8,128)(2,1)S(1)}, bf16[512,960]{0,1:T(8,128)(2,1)S(1)}, u32[]{:S(2)}, u32[]{:S(2)}) %collective-permute-start.8) | collective-permute-done | bytes 983072 | tf_op jit(solution)/shard_map/ppermute | solution.py:214
  141.4 20.5 %collective-permute-done.11 = bf16[512,960]{0,1:T(8,128)(2,1)} collective-permute-done((bf16[512,960]{0,1:T(8,128)(2,1)}, bf16[512,960]{0,1:T(8,128)(2,1)}, u32[]{:S(2)}, u32[]{:S(2)}) %collective-permute-start.11) | collective-permute-done | bytes 983072 | tf_op jit(solution)/shard_map/ppermute | solution.py:214
  164.2 17.7 %collective-permute-done.9 = bf16[512,960]{0,1:T(8,128)(2,1)} collective-permute-done((bf16[512,960]{0,1:T(8,128)(2,1)}, bf16[512,960]{0,1:T(8,128)(2,1)}, u32[]{:S(2)}, u32[]{:S(2)}) %collective-permute-start.9) | collective-permute-done | bytes 983072 | tf_op jit(solution)/shard_map/ppermute | solution.py:214
  182.0 3.7 multiply_add_fusion
  188.1 11.6 %shard_map.213 = (f32[15,64,512]{2,1,0:T(8,128)}, f32[5,64,1024]{2,1,0:T(8,128)S(1)}, f32[5,64,1024]{2,1,0:T(8,128)}) custom-call(s32[1]{0:T(128)} %bitcast.1.me_ref, s32[1024,1]{1,0:T(8,128)S(1)} %copy-done.7, s32[1,512]{1,0:T(1,128)S(1)} %constant_dynamic-slice_fusion.12.segq_ref, bf16[15,64,512]{2,1,0:T(8,128)(2,1)S(1)} %fusion.22.q_ref, ...), custom_call_target="tpu_custom_call" | custom-call | flops 20132659200 | bytes 10485760 | tf_op jit(solution)/shard_map/pallas_call | solution.py:194
  210.1 3.1 constant_dynamic-update-slice_fusion.7
  215.7 12.4 %collective-permute-done.12 = bf16[10,64,512]{2,1,0:T(8,128)(2,1)} collective-permute-done((bf16[10,64,512]{2,1,0:T(8,128)(2,1)}, bf16[10,64,512]{2,1,0:T(8,128)(2,1)}, u32[]{:S(2)}, u32[]{:S(2)}) %collective-permute-start.12) | collective-permute-done | bytes 655392 | tf_op jit(solution)/shard_map/ppermute | solution.py:406
  241.8 5.7 constant_dynamic-slice_fusion.7
  247.4 4.9 copy.67
  252.4 5.1 fusion.55
  257.5 3.7 fusion.56
  261.2 4.5 copy.66
  265.6 45.8 %collective-permute-done.13 = bf16[1344,960]{0,1:T(8,128)(2,1)} collective-permute-done((bf16[1344,960]{0,1:T(8,128)(2,1)}, bf16[1344,960]{0,1:T(8,128)(2,1)}, u32[]{:S(2)}, u32[]{:S(2)}) %collective-permute-start.13) | collective-permute-done | bytes 2580512 | tf_op jit(solution)/shard_map/ppermute | solution.py:214
  311.4 3.2 add.246
  318.5 5.5 fusion.57
  338.9 4.1 add_convert_fusion
  344.7 26.4 %collective-permute-done.21 = bf16[168,960]{0,1:T(8,128)(2,1)} collective-permute-done((bf16[168,960]{0,1:T(8,128)(2,1)S(1)}, bf16[168,960]{0,1:T(8,128)(2,1)}, u32[]{:S(2)}, u32[]{:S(2)}) %collective-permute-start.21) | collective-permute-done | bytes 322592 | tf_op jit(solution)/shard_map/ppermute | solution.py:214
  375.2 11.5 %collective-permute-done.22 = bf16[84,960]{0,1:T(8,128)(2,1)S(1)} collective-permute-done((bf16[84,960]{0,1:T(8,128)(2,1)S(1)}, bf16[84,960]{0,1:T(8,128)(2,1)S(1)}, u32[]{:S(2)}, u32[]{:S(2)}) %collective-permute-start.22) | collective-permute-done | bytes 161312 | tf_op jit(solution)/shard_map/ppermute | solution.py:214
  388.8 7.8 %collective-permute-done.16 = bf16[84,960]{0,1:T(8,128)(2,1)S(1)} collective-permute-done((bf16[84,960]{0,1:T(8,128)(2,1)S(1)}, bf16[84,960]{0,1:T(8,128)(2,1)S(1)}, u32[]{:S(2)}, u32[]{:S(2)}) %collective-permute-start.16) | collective-permute-done | bytes 161312 | tf_op jit(solution)/shard_map/ppermute | solution.py:214
  405.9 12.0 %collective-permute-done.17 = bf16[42,960]{0,1:T(8,128)(2,1)S(1)} collective-permute-done((bf16[42,960]{0,1:T(8,128)(2,1)S(1)}, bf16[42,960]{0,1:T(8,128)(2,1)S(1)}, u32[]{:S(2)}, u32[]{:S(2)}) %collective-permute-start.17) | collective-permute-done | bytes 80672 | tf_op jit(solution)/shard_map/ppermute | solution.py:214
  419.3 14.6 %collective-permute-done.18 = bf16[42,960]{0,1:T(8,128)(2,1)S(1)} collective-permute-done((bf16[42,960]{0,1:T(8,128)(2,1)S(1)}, bf16[42,960]{0,1:T(8,128)(2,1)S(1)}, u32[]{:S(2)}, u32[]{:S(2)}) %collective-permute-start.18) | collective-permute-done | bytes 80672 | tf_op jit(solution)/shard_map/ppermute | solution.py:214
  439.7 3.4 collective-permute-done.19
  445.5 19.1 %collective-permute-done.26 = bf16[168,960]{1,0:T(8,128)(2,1)S(1)} collective-permute-done((bf16[168,960]{1,0:T(8,128)(2,1)S(1)}, bf16[168,960]{1,0:T(8,128)(2,1)S(1)}, u32[]{:S(2)}, u32[]{:S(2)}) %collective-permute-start.26) | collective-permute-done | bytes 322592 | tf_op jit(solution)/shard_map/ppermute | solution.py:214
  471.2 70.3 %all-reduce.4.cloned.1.call-done = (bf16[1280,960]{0,1:T(8,128)(2,1)}, bf16[1280,960]{0,1:T(8,128)(2,1)}, bf16[1280,960]{0,1:T(8,128)(2,1)}) async-done(((bf16[1280,960]{0,1:T(8,128)(2,1)}, bf16[1280,960]{0,1:T(8,128)(2,1)}, bf16[1280,960]{0,1:T(8,128)(2,1)}), (bf16[1280,960]{0,1:T(8,128)(2,1)}, bf16[1280,960]{0,1:T(8,128)(2,1)}, bf16[1280,960]{0,1:T(8,128)(2,1)})) %all-reduce.4.cloned.1.call-update) | async-done | bytes 7372816 | tf_op jit(solution)/shard_map/psum | solution.py:385
  541.5 4.5 convert_element_type.216
  555.2 4.0 fusion.42
  (353 shorter events, 159.4 us)
Async XLA Ops:
  7.2 99.1 %copy-start = (bf16[1280,960]{0,1:T(8,128)(2,1)S(1)}, bf16[1280,960]{0,1:T(8,128)(2,1)}, u32[]{:S(2)}) copy-start(bf16[1280,960]{0,1:T(8,128)(2,1)} %param.25) | copy-start | bytes 7372804
  7.2 534.3 %all-reduce.4.cloned.1.call-start = ((), (), s32[]{:S(2)}) async-start(), calls=%async_computation | async-start | bytes 14745600 | tf_op jit(solution)/shard_map/psum | solution.py:385
  12.6 11.3 %collective-permute-start = (bf16[160,960]{1,0:T(8,128)(2,1)}, bf16[160,960]{1,0:T(8,128)(2,1)}, u32[]{:S(2)}, u32[]{:S(2)}) collective-permute-start(bf16[160,960]{1,0:T(8,128)(2,1)} %constant_dynamic-slice_fusion.11), channel_id=1, source_target_pairs={{0,16},{16,0},{1,17},{17,1},{2,18},{18,2},{3,19},{19,3},{4,20},{20... | collective-permute-start | bytes 921608 | tf_op jit(solution)/shard_map/ppermute | solution.py:214
  15.6 8.0 %collective-permute-start.4 = (bf16[480,2]{0,1:T(2,128)(2,1)S(1)}, bf16[480,2]{0,1:T(2,128)(2,1)S(1)}, u32[]{:S(2)}, u32[]{:S(2)}) collective-permute-start(bf16[480,2]{0,1:T(2,128)(2,1)S(1)} %pad_maximum_fusion.4), channel_id=1, source_target_pairs={{0,16},{16,0},{1,17},{17,1},{2,18},{18,2},{3,19},{19,3},{4,20},{20... | collective-permute-start | bytes 5768 | tf_op jit(solution)/shard_map/ppermute | solution.py:214
  23.9 1.9 collective-permute-start.1
  31.2 42.5 %collective-permute-start.5 = (bf16[10,64,512]{2,1,0:T(8,128)(2,1)}, bf16[10,64,512]{2,1,0:T(8,128)(2,1)}, u32[]{:S(2)}, u32[]{:S(2)}) collective-permute-start(bf16[10,64,512]{2,1,0:T(8,128)(2,1)} %pad_maximum_fusion.1), channel_id=1, source_target_pairs={{0,16},{1,17},{2,18},{3,19},{4,20},{5,21},{6,22},{7,23},{8,24},{9,... | collective-permute-start | bytes 1966088 | tf_op jit(solution)/shard_map/ppermute | solution.py:334
  36.8 24.0 %collective-permute-start.6 = (bf16[240,960]{1,0:T(8,128)(2,1)}, bf16[240,960]{1,0:T(8,128)(2,1)}, u32[]{:S(2)}, u32[]{:S(2)}) collective-permute-start(bf16[240,960]{1,0:T(8,128)(2,1)} %constant_dynamic-slice_fusion.9), channel_id=1, source_target_pairs={{0,16},{16,0},{1,17},{17,1},{2,18},{18,2},{3,19},{19,3},{4,20},{20... | collective-permute-start | bytes 1382408 | tf_op jit(solution)/shard_map/ppermute | solution.py:214
  37.6 33.7 %collective-permute-start.2 = (bf16[240,960]{1,0:T(8,128)(2,1)}, bf16[240,960]{1,0:T(8,128)(2,1)}, u32[]{:S(2)}, u32[]{:S(2)}) collective-permute-start(bf16[240,960]{1,0:T(8,128)(2,1)} %constant_dynamic-slice_fusion.10), channel_id=1, source_target_pairs={{0,16},{16,0},{1,17},{17,1},{2,18},{18,2},{3,19},{19,3},{4,20},{20... | collective-permute-start | bytes 1382408 | tf_op jit(solution)/shard_map/ppermute | solution.py:214
  44.9 85.3 %collective-permute-start.10 = (bf16[512,960]{0,1:T(8,128)(2,1)}, bf16[512,960]{0,1:T(8,128)(2,1)S(1)}, u32[]{:S(2)}, u32[]{:S(2)}) collective-permute-start(bf16[512,960]{0,1:T(8,128)(2,1)} %bitcast.14), channel_id=1, source_target_pairs={{0,16},{16,0},{1,17},{17,1},{2,18},{18,2},{3,19},{19,3},{4,20},{20... | collective-permute-start | bytes 2949128 | tf_op jit(solution)/shard_map/ppermute | solution.py:214
  60.8 13.3 %collective-permute-start.7 = (bf16[240,960]{1,0:T(8,128)(2,1)}, bf16[240,960]{1,0:T(8,128)(2,1)S(1)}, u32[]{:S(2)}, u32[]{:S(2)}) collective-permute-start(bf16[240,960]{1,0:T(8,128)(2,1)} %collective-permute-done.6), channel_id=1, source_target_pairs={{0,1},{1,0},{2,3},{3,2},{4,5},{5,4},{6,7},{7,6},{8,9},{9,8},{10,11... | collective-permute-start | bytes 1382408 | tf_op jit(solution)/shard_map/ppermute | solution.py:214
  71.3 2.9 collective-permute-start.3
  91.7 35.5 %collective-permute-start.8 = (bf16[512,960]{0,1:T(8,128)(2,1)S(1)}, bf16[512,960]{0,1:T(8,128)(2,1)S(1)}, u32[]{:S(2)}, u32[]{:S(2)}) collective-permute-start(bf16[512,960]{0,1:T(8,128)(2,1)S(1)} %multiply_convert_fusion.6), channel_id=1, source_target_pairs={{0,16},{16,0},{1,17},{17,1},{2,18},{18,2},{3,19},{19,3},{4,20},{20... | collective-permute-start | bytes 2949128 | tf_op jit(solution)/shard_map/ppermute | solution.py:214
  137.0 24.9 %collective-permute-start.11 = (bf16[512,960]{0,1:T(8,128)(2,1)}, bf16[512,960]{0,1:T(8,128)(2,1)}, u32[]{:S(2)}, u32[]{:S(2)}) collective-permute-start(bf16[512,960]{0,1:T(8,128)(2,1)} %add_convert_fusion.3), channel_id=1, source_target_pairs={{0,16},{16,0},{1,17},{17,1},{2,18},{18,2},{3,19},{19,3},{4,20},{20... | collective-permute-start | bytes 2949128 | tf_op jit(solution)/shard_map/ppermute | solution.py:214
  141.1 40.8 %collective-permute-start.9 = (bf16[512,960]{0,1:T(8,128)(2,1)}, bf16[512,960]{0,1:T(8,128)(2,1)}, u32[]{:S(2)}, u32[]{:S(2)}) collective-permute-start(bf16[512,960]{0,1:T(8,128)(2,1)} %convolution_convert_fusion.4), channel_id=1, source_target_pairs={{0,16},{16,0},{1,17},{17,1},{2,18},{18,2},{3,19},{19,3},{4,20},{20... | collective-permute-start | bytes 2949128 | tf_op jit(solution)/shard_map/ppermute | solution.py:214
  141.4 40.5 %copy-start.30 = (bf16[512,960]{0,1:T(8,128)(2,1)S(1)}, bf16[512,960]{0,1:T(8,128)(2,1)}, u32[]{:S(2)}) copy-start(bf16[512,960]{0,1:T(8,128)(2,1)} %add_convert_fusion.5) | copy-start | bytes 2949124
  141.4 40.5 %copy-start.68 = (bf16[512,960]{0,1:T(8,128)(2,1)S(1)}, bf16[512,960]{0,1:T(8,128)(2,1)}, u32[]{:S(2)}) copy-start(bf16[512,960]{0,1:T(8,128)(2,1)} %convolution_convert_fusion.5) | copy-start | bytes 2949124
  203.6 24.5 %collective-permute-start.12 = (bf16[10,64,512]{2,1,0:T(8,128)(2,1)}, bf16[10,64,512]{2,1,0:T(8,128)(2,1)}, u32[]{:S(2)}, u32[]{:S(2)}) collective-permute-start(bf16[10,64,512]{2,1,0:T(8,128)(2,1)} %slice.153), channel_id=1, source_target_pairs={{16,0},{17,1},{18,2},{19,3},{20,4},{21,5},{22,6},{23,7},{24,8},{25... | collective-permute-start | bytes 1966088 | tf_op jit(solution)/shard_map/ppermute | solution.py:406
  252.4 59.0 %collective-permute-start.13 = (bf16[1344,960]{0,1:T(8,128)(2,1)}, bf16[1344,960]{0,1:T(8,128)(2,1)}, u32[]{:S(2)}, u32[]{:S(2)}) collective-permute-start(bf16[1344,960]{0,1:T(8,128)(2,1)} %copy.67), channel_id=1, source_target_pairs={{0,16},{16,0},{1,17},{17,1},{2,18},{18,2},{3,19},{19,3},{4,20},{20... | collective-permute-start | bytes 7741448 | tf_op jit(solution)/shard_map/ppermute | solution.py:214
  318.5 11.4 %collective-permute-start.14 = (bf16[672,960]{1,0:T(8,128)(2,1)}, bf16[672,960]{1,0:T(8,128)(2,1)S(1)}, u32[]{:S(2)}, u32[]{:S(2)}) collective-permute-start(bf16[672,960]{1,0:T(8,128)(2,1)} %copy.59), channel_id=1, source_target_pairs={{0,1},{1,0},{2,3},{3,2},{4,5},{5,4},{6,7},{7,6},{8,9},{9,8},{10,11... | collective-permute-start | bytes 3870728 | tf_op jit(solution)/shard_map/ppermute | solution.py:214
  336.2 35.0 %collective-permute-start.21 = (bf16[168,960]{0,1:T(8,128)(2,1)S(1)}, bf16[168,960]{0,1:T(8,128)(2,1)}, u32[]{:S(2)}, u32[]{:S(2)}) collective-permute-start(bf16[168,960]{0,1:T(8,128)(2,1)S(1)} %constant_dynamic-slice_fusion.2), channel_id=1, source_target_pairs={{0,8},{1,9},{2,10},{3,11},{4,12},{5,13},{6,14},{7,15},{8,0},{9,1},... | collective-permute-start | bytes 967688 | tf_op jit(solution)/shard_map/ppermute | solution.py:214
  343.2 30.6 %collective-permute-start.15 = (bf16[168,960]{0,1:T(8,128)(2,1)S(1)}, bf16[168,960]{0,1:T(8,128)(2,1)S(1)}, u32[]{:S(2)}, u32[]{:S(2)}) collective-permute-start(bf16[168,960]{0,1:T(8,128)(2,1)S(1)} %constant_dynamic-slice_fusion.5), channel_id=1, source_target_pairs={{0,2},{1,3},{2,0},{3,1},{4,6},{5,7},{6,4},{7,5},{8,10},{9,11},{10,... | collective-permute-start | bytes 967688 | tf_op jit(solution)/shard_map/ppermute | solution.py:214
  372.6 14.1 %collective-permute-start.22 = (bf16[84,960]{0,1:T(8,128)(2,1)S(1)}, bf16[84,960]{0,1:T(8,128)(2,1)S(1)}, u32[]{:S(2)}, u32[]{:S(2)}) collective-permute-start(bf16[84,960]{0,1:T(8,128)(2,1)S(1)} %constant_dynamic-slice_fusion.1), channel_id=1, source_target_pairs={{0,4},{1,5},{2,6},{3,7},{4,0},{5,1},{6,2},{7,3},{8,12},{9,13},{10,... | collective-permute-start | bytes 483848 | tf_op jit(solution)/shard_map/ppermute | solution.py:214
  374.3 22.3 %collective-permute-start.16 = (bf16[84,960]{0,1:T(8,128)(2,1)S(1)}, bf16[84,960]{0,1:T(8,128)(2,1)S(1)}, u32[]{:S(2)}, u32[]{:S(2)}) collective-permute-start(bf16[84,960]{0,1:T(8,128)(2,1)S(1)} %constant_dynamic-slice_fusion.4), channel_id=1, source_target_pairs={{0,4},{1,5},{2,6},{3,7},{4,0},{5,1},{6,2},{7,3},{8,12},{9,13},{10,... | collective-permute-start | bytes 483848 | tf_op jit(solution)/shard_map/ppermute | solution.py:214
  387.0 9.7 %collective-permute-start.23 = (bf16[42,960]{0,1:T(8,128)(2,1)S(1)}, bf16[42,960]{0,1:T(8,128)(2,1)S(1)}, u32[]{:S(2)}, u32[]{:S(2)}) collective-permute-start(bf16[42,960]{0,1:T(8,128)(2,1)S(1)} %constant_dynamic-slice_fusion), channel_id=1, source_target_pairs={{0,2},{1,3},{2,0},{3,1},{4,6},{5,7},{6,4},{7,5},{8,10},{9,11},{10,... | collective-permute-start | bytes 241928 | tf_op jit(solution)/shard_map/ppermute | solution.py:214
  396.9 6.3 %collective-permute-start.24 = (bf16[42,960]{0,1:T(8,128)(2,1)S(1)}, bf16[42,960]{0,1:T(8,128)(2,1)S(1)}, u32[]{:S(2)}, u32[]{:S(2)}) collective-permute-start(bf16[42,960]{0,1:T(8,128)(2,1)S(1)} %dynamic-slice_add_fusion.3), channel_id=1, source_target_pairs={{0,2},{1,3},{2,0},{3,1},{4,6},{5,7},{6,4},{7,5},{8,10},{9,11},{10,... | collective-permute-start | bytes 241928 | tf_op jit(solution)/shard_map/ppermute | solution.py:214
  398.8 19.2 %collective-permute-start.17 = (bf16[42,960]{0,1:T(8,128)(2,1)S(1)}, bf16[42,960]{0,1:T(8,128)(2,1)S(1)}, u32[]{:S(2)}, u32[]{:S(2)}) collective-permute-start(bf16[42,960]{0,1:T(8,128)(2,1)S(1)} %constant_dynamic-slice_fusion.3), channel_id=1, source_target_pairs={{0,8},{1,9},{2,10},{3,11},{4,12},{5,13},{6,14},{7,15},{8,0},{9,1},... | collective-permute-start | bytes 241928 | tf_op jit(solution)/shard_map/ppermute | solution.py:214
  403.9 32.1 %collective-permute-start.25 = (bf16[84,960]{1,0:T(8,128)(2,1)S(1)}, bf16[84,960]{1,0:T(8,128)(2,1)S(1)}, u32[]{:S(2)}, u32[]{:S(2)}) collective-permute-start(bf16[84,960]{1,0:T(8,128)(2,1)S(1)} %dynamic_update_slice.105), channel_id=1, source_target_pairs={{0,4},{1,5},{2,6},{3,7},{4,0},{5,1},{6,2},{7,3},{8,12},{9,13},{10,... | collective-permute-start | bytes 483848 | tf_op jit(solution)/shard_map/ppermute | solution.py:214
  418.1 15.8 %collective-permute-start.18 = (bf16[42,960]{0,1:T(8,128)(2,1)S(1)}, bf16[42,960]{0,1:T(8,128)(2,1)S(1)}, u32[]{:S(2)}, u32[]{:S(2)}) collective-permute-start(bf16[42,960]{0,1:T(8,128)(2,1)S(1)} %dynamic-slice_add_fusion.5), channel_id=1, source_target_pairs={{0,8},{1,9},{2,10},{3,11},{4,12},{5,13},{6,14},{7,15},{8,0},{9,1},... | collective-permute-start | bytes 241928 | tf_op jit(solution)/shard_map/ppermute | solution.py:214
  434.7 8.4 %collective-permute-start.19 = (bf16[84,960]{1,0:T(8,128)(2,1)S(1)}, bf16[84,960]{1,0:T(8,128)(2,1)S(1)}, u32[]{:S(2)}, u32[]{:S(2)}) collective-permute-start(bf16[84,960]{1,0:T(8,128)(2,1)S(1)} %dynamic_update_slice.99), channel_id=1, source_target_pairs={{0,4},{1,5},{2,6},{3,7},{4,0},{5,1},{6,2},{7,3},{8,12},{9,13},{10,... | collective-permute-start | bytes 483848 | tf_op jit(solution)/shard_map/ppermute | solution.py:214
  437.0 27.6 %collective-permute-start.26 = (bf16[168,960]{1,0:T(8,128)(2,1)S(1)}, bf16[168,960]{1,0:T(8,128)(2,1)S(1)}, u32[]{:S(2)}, u32[]{:S(2)}) collective-permute-start(bf16[168,960]{1,0:T(8,128)(2,1)S(1)} %dynamic_update_slice.107), channel_id=1, source_target_pairs={{0,8},{1,9},{2,10},{3,11},{4,12},{5,13},{6,14},{7,15},{8,0},{9,1},... | collective-permute-start | bytes 967688 | tf_op jit(solution)/shard_map/ppermute | solution.py:214
  443.9 20.7 %collective-permute-start.20 = (bf16[168,960]{1,0:T(8,128)(2,1)S(1)}, bf16[168,960]{1,0:T(8,128)(2,1)S(1)}, u32[]{:S(2)}, u32[]{:S(2)}) collective-permute-start(bf16[168,960]{1,0:T(8,128)(2,1)S(1)} %dynamic_update_slice.101), channel_id=1, source_target_pairs={{0,2},{1,3},{2,0},{3,1},{4,6},{5,7},{6,4},{7,5},{8,10},{9,11},{10,... | collective-permute-start | bytes 967688 | tf_op jit(solution)/shard_map/ppermute | solution.py:214
  468.5 82.8 %collective-permute-start.27 = (bf16[672,960]{1,0:T(8,128)(2,1)}, bf16[672,960]{1,0:T(8,128)(2,1)}, u32[]{:S(2)}, u32[]{:S(2)}) collective-permute-start(bf16[672,960]{1,0:T(8,128)(2,1)} %get-tuple-element.82), channel_id=1, source_target_pairs={{0,1},{1,0},{2,3},{3,2},{4,5},{5,4},{6,7},{7,6},{8,9},{9,8},{10,11... | collective-permute-start | bytes 3870728 | tf_op jit(solution)/shard_map/ppermute | solution.py:214
  (78 other events, 413.6 us)
Sparse Core Ops, SparseCore 0:
  343.1 198.3 all-reduce.3
